TPU v7x, 256 devices: a whole 4x4x8 slice. The times are simulated.
256 devices in a mesh: grp: 4 (over x), mem: 64 (over z, y, core).
Axes of the slice: x: 4, y: 4, z: 8, core: 2. Of those that a mesh axis runs over, the one named last changes fastest.
Arguments:
- bank: bfloat16 [196608, 1024], P(('grp', 'mem')), may hold values from -1 to 1
- pattern: int32 [1536, 384], P(('grp', 'mem')), may hold values from 0 to 1, as said below
- pair_list: int32 [256, 4, 4], P(('grp', 'mem')), may hold values from 0 to 5, as said below
- pair_count: int32 [256, 4], P(('grp', 'mem')), may hold values from 0 to 4, as said below
Outputs:
- coarse_best: float32 [196608], P(('grp', 'mem'))
- fine_best: float32 [196608], P(('grp', 'mem'))
Inputs may be any that keep to these rules, and one draw needn't show every extreme that they name: pattern is symmetric inside each group's 384 x 384 block and 1 on its diagonal. `pair_list`: values in slots at or beyond pair_count, and in a device's own group, are not read; a block may be listed more than once. `pair_count`: zero for a device's own group; every device has a live slot; for one member index drawn from the seed, every device of that index has 4 live slots toward every other group.
All inputs are finite; a program needn't handle non-finite values.
Results may differ from a plain program's by a relative error of at most 0.0003.
Values may be sent and summed in bfloat16 or wider, within the bound.
A program may use at most 64 MiB of HBM per device.

v0:
```python
import jax
import jax.numpy as jnp
from jax import lax
from jax.sharding import PartitionSpec as P

PREF = 64
BLK = 128


NEG = -1e30


def tile_maxima(own_pref, own_patt, row_base, cols):
    count = cols.shape[0]
    col_ids = jnp.arange(count, dtype=jnp.int32)
    blocks_per = 256 // BLK

    def one_tile(inputs):
        block, pblock, which = inputs
        scores = lax.dot_general(
            block, cols, (((1,), (1,)), ((), ())), preferred_element_type=jnp.float32
        )
        keep = jnp.broadcast_to(
            pblock[:, None, :, None] > 0, (blocks_per, BLK, count // BLK, BLK)
        ).reshape(256, count)
        row_ids = row_base + which * 256 + jnp.arange(256, dtype=jnp.int32)
        keep = keep & (row_ids[:, None] != col_ids[None, :])
        masked = jnp.where(keep, scores, NEG)
        return (jnp.max(masked, axis=1), jnp.max(masked, axis=0))

    tiles = own_pref.shape[0]
    row_best, col_best = lax.map(one_tile, (own_pref, own_patt, jnp.arange(tiles, dtype=jnp.int32)))
    return (row_best.reshape(-1), jnp.max(col_best, axis=0))


def per_device(bank, pattern, pair_list, pair_count):
    rows_dev = bank.shape[0]
    groups = lax.axis_size("grp")
    member = lax.axis_index("mem")
    own_base = member * rows_dev
    prefix = bank[:, :PREF]
    own_pref = prefix.reshape(rows_dev // 256, 256, PREF)
    own_patt = pattern.reshape(rows_dev // 256, 256 // BLK, pattern.shape[1])
    packed = prefix.reshape(-1, 128)
    cols = lax.all_gather(packed, "mem", axis=0, tiled=True).reshape(-1, PREF)
    row_best, unused = tile_maxima(own_pref, own_patt, own_base, cols)
    coarse = jnp.maximum(jnp.full((rows_dev,), NEG, jnp.float32), row_best)
    slots = pair_list.shape[2]
    asked = pair_list.reshape(groups, slots)
    live = pair_count.reshape(groups, 1)
    ids_in, live_in = (
        lax.all_to_all(asked, "grp", split_axis=0, concat_axis=0, tiled=True),
        lax.all_to_all(live, "grp", split_axis=0, concat_axis=0, tiled=True),
    )
    local_blocks = bank.reshape(rows_dev // BLK, BLK, bank.shape[1])
    outgoing = local_blocks[ids_in]
    fetched = lax.all_to_all(outgoing, "grp", split_axis=0, concat_axis=0, tiled=True)
    shape = fetched.shape
    flat = fetched.reshape(shape[0] * shape[1], BLK, shape[3])

    def one_block(block):
        scores = lax.dot_general(
            bank, block, (((1,), (1,)), ((), ())), preferred_element_type=jnp.float32
        )
        return (jnp.max(scores, axis=0), jnp.max(scores, axis=1))

    col_part, row_part = lax.map(one_block, flat)
    col_all = col_part.reshape(shape[0], shape[1], BLK)
    row_all = row_part.reshape(shape[0], shape[1], rows_dev)
    own_group = lax.axis_index("grp")
    valid = (jnp.arange(slots, dtype=jnp.int32)[None, :] < live) & (
        jnp.arange(groups, dtype=jnp.int32)[:, None] != own_group
    )
    fine = jnp.max(jnp.where(valid[:, :, None], row_all, NEG), axis=(0, 1))
    col_masked = jnp.where(valid[:, :, None], col_all, NEG)
    returned_cols = lax.all_to_all(col_masked, "grp", split_axis=0, concat_axis=0, tiled=True)
    onehot = ids_in[:, :, None] == jnp.arange(rows_dev // BLK, dtype=jnp.int32)[None, None, :]
    merged = jnp.max(
        jnp.where(onehot[:, :, :, None], returned_cols[:, :, None, :], NEG), axis=(0, 1)
    )
    fine = jnp.maximum(fine, merged.reshape(-1))
    return (coarse, fine)


def solution(mesh):
    return jax.shard_map(
        per_device,
        mesh=mesh,
        in_specs=(
            P(("grp", "mem"), None),
            P(("grp", "mem"), None),
            P(("grp", "mem"), None, None),
            P(("grp", "mem"), None),
        ),
        out_specs=(P(("grp", "mem")), P(("grp", "mem"))),
        check_vma=False,
    )
```

profile of v0, /device:TPU:1, one launch (start us, length us, event | category | flops | bytes accessed | tf_op | source)
XLA Modules:
  0.0 285.2 jit_solution(10839136191148721526)
XLA Ops:
  9.1 8.9 %all_to_all.22 = s32[4,1,4]{2,1,0:T(1,128)S(1)} all-to-all(s32[4,1,4]{2,1,0:T(1,128)} %bitcast.65), channel_id=1, replica_groups=mesh['grp'=4,'mem'=64] {'grp'}, dimensions={0} | all-to-all | bytes 128 | tf_op jit(solution)/shard_map/all_to_all | solution.py:52
  18.1 4.2 %gather_fusion = bf16[16,128,1024]{2,1,0:T(8,128)(2,1)} fusion(bf16[6,128,1024]{2,1,0:T(8,128)(2,1)} %bitcast.57, s32[1024]{0:T(1024)S(1)} %pad_clamp_fusion), kind=kCustom, calls=%fused_computation | custom fusion | bytes 8388672 | tf_op jit(solution)/shard_map/gather | solution.py:56
  22.3 4.9 %all-to-all-start.1 = ((bf16[4,4,128,1024]{3,2,1,0:T(8,128)(2,1)}), bf16[4,4,128,1024]{3,2,1,0:T(8,128)(2,1)}, u32[]{:S(2)}, u32[]{:S(2)}) async-start(bf16[4,4,128,1024]{3,2,1,0:T(8,128)(2,1)} %bitcast.58), calls=%async_computation.1 | async-start | bytes 8388608 | tf_op jit(solution)/shard_map/all_to_all | solution.py:57
  27.4 45.9 %all-to-all-done.1 = bf16[4,4,128,1024]{3,2,1,0:T(8,128)(2,1)} async-done(((bf16[4,4,128,1024]{3,2,1,0:T(8,128)(2,1)}), bf16[4,4,128,1024]{3,2,1,0:T(8,128)(2,1)}, u32[]{:S(2)}, u32[]{:S(2)}) %all-to-all-start.1) | async-done | bytes 4194336 | tf_op jit(solution)/shard_map/all_to_all | solution.py:57
  73.3 29.6 %while.23 = (s32[]{:T(128)}, f32[16,128]{1,0:T(8,128)S(1)}, f32[16,768]{1,0:T(8,128)S(1)}, bf16[16,128,1024]{2,1,0:T(8,128)(2,1)}, bf16[768,1024]{1,0:T(8,128)(2,1)S(1)}, /*index=5*/s32[]{:T(128)}, s32[]{:T(128)}) while((s32[]{:T(128)}, f32[16,128]{1,0:T(8,128)S(1)}, f32[16,768]{1,0:T(8,128)S(1)}, bf16[16,128,1024]{2,1,0:T(8,128)(2,1)}, ...), condition=%wide.region_6.7_spmd, body=%wide.region_3.6_spmd.sunk | while | flops 201522304 | bytes 1852001 | solution.py:67
  75.1 1.7 fusion.21
  77.0 1.7 fusion.21
  78.9 1.7 fusion.21
  80.7 1.7 fusion.21
  82.6 1.7 fusion.21
  84.4 1.7 fusion.21
  86.3 1.7 fusion.21
  88.1 1.7 fusion.21
  93.7 1.7 fusion.21
  103.5 3.2 %all-to-all-start.2 = ((f32[4,4,128]{2,1,0:T(4,128)}), f32[4,4,128]{2,1,0:T(4,128)S(1)}, u32[]{:S(2)}, u32[]{:S(2)}) async-start(f32[4,4,128]{2,1,0:T(4,128)} %broadcast_select_fusion), calls=%async_computation.2 | async-start | bytes 16384 | tf_op jit(solution)/shard_map/all_to_all | solution.py:76
  106.9 4.0 %all-to-all-done.2 = f32[4,4,128]{2,1,0:T(4,128)S(1)} async-done(((f32[4,4,128]{2,1,0:T(4,128)}), f32[4,4,128]{2,1,0:T(4,128)S(1)}, u32[]{:S(2)}, u32[]{:S(2)}) %all-to-all-start.2) | async-done | bytes 8224 | tf_op jit(solution)/shard_map/all_to_all | solution.py:76
  111.6 16.0 %reshape.144 = bf16[49152,64]{1,0:T(8,128)(2,1)} reshape(bf16[24576,128]{1,0:T(8,128)(2,1)} %all-gather.2.cloned.1.call-done) | data formatting | bytes 12582912 | tf_op jit(solution)/shard_map/reshape | solution.py:45
  127.7 150.1 %while.24 = (s32[]{:T(128)}, f32[3,256]{1,0:T(4,128)S(1)}, s32[3,2,384]{2,1,0:T(2,128)S(1)}, s32[3]{0:T(128)S(1)}, s32[]{:T(128)}, /*index=5*/bf16[3,256,64]{2,1...) while((s32[]{:T(128)}, f32[3,256]{1,0:T(4,128)S(1)}, ...), condition=%wide.region_2.3_spmd.clone, body=%wide.region_0.2_spmd.clone.sunk | while | flops 1660945152 | bytes 31532704 | solution.py:32
  128.9 7.3 %broadcast_in_dim.119 = pred[2,128,384,128]{3,2,1,0:T(32,128)(4,1)S(1)} broadcast(pred[2,384]{1,0:T(4,128)(4,1)S(1)} %compare_bitcast_fusion.2), dimensions={0,2} | broadcast | bytes 12583680 | tf_op jit(solution)/shard_map/while/body/eval_jaxpr/broadcast_in_dim | solution.py:23
  136.2 41.5 %fusion.24 = f32[256]{0:T(256)S(1)} fusion(bf16[49152,64]{1,0:T(8,128)(2,1)} %get-tuple-element.221, s32[256]{0:T(256)S(1)} %iota_add_fusion.2, pred[32,8,384,128]{3,2,1,0:T(32,128)(4,1)S(1)} %bitcast.56, bf16[3,256,64]{2,1,0:T(8,128)(2,1)S(1)} %get-tuple-element.220, s32[]{:T(128)S(6)} %copy.19), kind=kOutput, calls=%fused_computation.9.clone.1 | convolution fusion | flops 1660944128 | bytes 18941956 | tf_op jit(solution)/shard_map/while/body/eval_jaxpr/dot_general | solution.py:20
  179.0 7.3 %broadcast_in_dim.119 = pred[2,128,384,128]{3,2,1,0:T(32,128)(4,1)S(1)} broadcast(pred[2,384]{1,0:T(4,128)(4,1)S(1)} %compare_bitcast_fusion.2), dimensions={0,2} | broadcast | bytes 12583680 | tf_op jit(solution)/shard_map/while/body/eval_jaxpr/broadcast_in_dim | solution.py:23
  186.3 41.4 %fusion.24 = f32[256]{0:T(256)S(1)} fusion(bf16[49152,64]{1,0:T(8,128)(2,1)} %get-tuple-element.221, s32[256]{0:T(256)S(1)} %iota_add_fusion.2, pred[32,8,384,128]{3,2,1,0:T(32,128)(4,1)S(1)} %bitcast.56, bf16[3,256,64]{2,1,0:T(8,128)(2,1)S(1)} %get-tuple-element.220, s32[]{:T(128)S(6)} %copy.19), kind=kOutput, calls=%fused_computation.9.clone.1 | convolution fusion | flops 1660944128 | bytes 18941956 | tf_op jit(solution)/shard_map/while/body/eval_jaxpr/dot_general | solution.py:20
  229.0 7.3 %broadcast_in_dim.119 = pred[2,128,384,128]{3,2,1,0:T(32,128)(4,1)S(1)} broadcast(pred[2,384]{1,0:T(4,128)(4,1)S(1)} %compare_bitcast_fusion.2), dimensions={0,2} | broadcast | bytes 12583680 | tf_op jit(solution)/shard_map/while/body/eval_jaxpr/broadcast_in_dim | solution.py:23
  236.3 41.4 %fusion.24 = f32[256]{0:T(256)S(1)} fusion(bf16[49152,64]{1,0:T(8,128)(2,1)} %get-tuple-element.221, s32[256]{0:T(256)S(1)} %iota_add_fusion.2, pred[32,8,384,128]{3,2,1,0:T(32,128)(4,1)S(1)} %bitcast.56, bf16[3,256,64]{2,1,0:T(8,128)(2,1)S(1)} %get-tuple-element.220, s32[]{:T(128)S(6)} %copy.19), kind=kOutput, calls=%fused_computation.9.clone.1 | convolution fusion | flops 1660944128 | bytes 18941956 | tf_op jit(solution)/shard_map/while/body/eval_jaxpr/dot_general | solution.py:20
  (96 shorter events, 20.1 us)
Async XLA Ops:
  7.2 66.1 %copy-start = (bf16[768,1024]{1,0:T(8,128)(2,1)S(1)}, bf16[768,1024]{1,0:T(8,128)(2,1)}, u32[]{:S(2)}) copy-start(bf16[768,1024]{1,0:T(8,128)(2,1)} %param.8) | copy-start | bytes 4718596
  7.2 20.0 %copy-start.1 = (s32[6,384]{1,0:T(8,128)S(1)}, s32[6,384]{1,0:T(8,128)}, u32[]{:S(2)}) copy-start(s32[6,384]{1,0:T(8,128)} %param.9) | copy-start | bytes 27652
  7.2 20.0 %copy-start.2 = (s32[1,4]{1,0:T(1,128)S(1)}, s32[1,4]{1,0:T(1,128)}, u32[]{:S(2)}) copy-start(s32[1,4]{1,0:T(1,128)} %param.11) | copy-start | bytes 52
  7.2 104.4 %all-gather.2.cloned.1.call-start = ((), (), s32[]{:S(2)}) async-start(), calls=%async_computation.3 | async-start | bytes 6389760 | tf_op jit(solution)/shard_map/all_gather | solution.py:45
  22.3 51.0 %all-to-all-start.1 = ((bf16[4,4,128,1024]{3,2,1,0:T(8,128)(2,1)}), bf16[4,4,128,1024]{3,2,1,0:T(8,128)(2,1)}, u32[]{:S(2)}, u32[]{:S(2)}) async-start(bf16[4,4,128,1024]{3,2,1,0:T(8,128)(2,1)} %bitcast.58), calls=%async_computation.1 | async-start | bytes 8388608 | tf_op jit(solution)/shard_map/all_to_all | solution.py:57
  103.5 7.4 %all-to-all-start.2 = ((f32[4,4,128]{2,1,0:T(4,128)}), f32[4,4,128]{2,1,0:T(4,128)S(1)}, u32[]{:S(2)}, u32[]{:S(2)}) async-start(f32[4,4,128]{2,1,0:T(4,128)} %broadcast_select_fusion), calls=%async_computation.2 | async-start | bytes 16384 | tf_op jit(solution)/shard_map/all_to_all | solution.py:76
Sparse Core Ops, SparseCore 0:
  10.8 85.4 all-gather.1
where the time goes:
time: 290 us; the launch traced here: 285 us
  matrix products  151 us (52%)
  waiting for transfers between devices  49.9 us (17%)
  local copies, waits for them, and re-layouts  48.6 us (17%)
  between operations  14.2 us (5%)
  blocking collectives  8.88 us (3%)
  starting transfers between devices  8.14 us (3%)
    dot_general x3, matrix products, one_tile(): lax.dot_general(block, cols, (((1,), (1,)), ((), ())), preferred_element_...  124 us
    all_to_all x1, waiting for transfers between devices, per_device(): lax.all_to_all(outgoing, 'grp', split_axis=0, concat_axis=0, tiled=True)  45.9 us
    dot_general x16, matrix products, one_block(): lax.dot_general(bank, block, (((1,), (1,)), ((), ())), preferred_element_...  27.1 us
    broadcast_in_dim x3, local copies, waits for them, and re-layouts, one_tile(): jnp.broadcast_to(pblock[:, None, :, None] > 0, (blocks_per, BLK, count //...  21.8 us
    reshape x1, local copies, waits for them, and re-layouts, per_device(): cols = lax.all_gather(packed, 'mem', axis=0, tiled=True).reshape(-1, PREF)  16 us
    all_to_all x1, blocking collectives, per_device(): lax.all_to_all(asked, 'grp', split_axis=0, concat_axis=0, tiled=True)  8.88 us
  transfers between devices with their start and end apart: 3, of which 2 were waited for; matrix products, arithmetic and copies ran while one was open for 12% of the time, Pallas kernels for 0%

commit v1 on v0

v1 whole, which is shorter than its diff:
```python
import functools

import jax
import jax.numpy as jnp
from jax import lax
from jax.experimental import pallas as pl
from jax.experimental.pallas import tpu as pltpu
from jax.sharding import PartitionSpec as P

PREF = 64
BLK = 128
NEG = -1e30
MESH = pl.DeviceIdType.MESH
COVERS = {64: (0, 1, 63, 58, 15, 41, 13, 4, 33), 4: (0, 1, 2)}


def dot_nt(a, b):
    return lax.dot_general(a, b, (((1,), (1,)), ((), ())), preferred_element_type=jnp.float32)


def kernel(
    cover, groups, members,
    bank, patt, plist, pcount,
    coarse, fine,
    own, pre, prev, lbuf, lsend, recv, lhs, rhs, racc, cacc, cret,
    pattpad, sel, ids, ids_s, f_own, f_prev, f_l, r2s, r1, r2,
    loc_sem, id_send, id_recv, c_send, c_recv, a_send, a_recv, l_send, l_recv, b_send, b_recv, r_send, r_recv,
):
    g = lax.axis_index("grp")
    m = lax.axis_index("mem")
    core = lax.rem(m, 2)
    nxt = lax.rem(g + 1 + 2 * core, groups)
    prv = lax.rem(g + 3 - 2 * core, groups)
    opp = lax.rem(g + 2, groups)
    slots = len(cover)
    rows = own.shape[0]
    half = rows // 2
    blocks = rows // BLK
    cap = lbuf.shape[0] // BLK
    to_user = [None] + [lax.rem(m + members - d, members) for d in cover[1:]]
    to_owner = [None] + [lax.rem(m + d, members) for d in cover[1:]]

    pre_copy = pltpu.make_async_copy(bank.at[:, pl.ds(0, 128)], pre, loc_sem.at[0])
    pre_copy.start()
    own_copy = pltpu.make_async_copy(bank, own, loc_sem.at[1])
    own_copy.start()

    barrier = pltpu.get_barrier_semaphore()
    for other in (nxt, prv, opp):
        pl.semaphore_signal(barrier, inc=1, device_id=(other, m), device_id_type=MESH)
    for k in range(1, slots):
        for other in (to_user[k], to_owner[k]):
            pl.semaphore_signal(barrier, inc=1, device_id=(g, other), device_id_type=MESH)

    lane = lax.broadcasted_iota(jnp.int32, (1, 128), 1)
    low = (lane < PREF).astype(jnp.float32)

    ids[0] = jnp.zeros((8, 128), jnp.int32)
    ids[0, 0:4, 0:4] = plist[0]
    ids[0, 4:5, 0:4] = pcount[...]
    pattpad[...] = jnp.zeros_like(pattpad)
    pattpad[0:blocks, :] = patt[...]
    for t in range(3):
        recv[0, half + 16 * t : half + 16 * t + 16, :] = (
            pattpad[:, 128 * t : 128 * t + 128].astype(jnp.float32).astype(jnp.bfloat16)
        )
    pre_copy.wait()
    recv[0, 0:half, :] = (
        pre[0:half, :].astype(jnp.float32) * low
        + pltpu.roll(pre[half:rows, :].astype(jnp.float32) * low, PREF, 1)
    ).astype(jnp.bfloat16)

    pl.semaphore_wait(barrier, 3 + 2 * (slots - 1))

    def remote(src, dst, send, rcv, where):
        copy = pltpu.make_async_remote_copy(
            src_ref=src, dst_ref=dst, send_sem=send, recv_sem=rcv, device_id=where, device_id_type=MESH
        )
        copy.start()
        return copy

    id_copies = [
        remote(ids.at[0], ids.at[1], id_send.at[0], id_recv.at[0], (nxt, m)),
        remote(ids.at[0], ids.at[2], id_send.at[1], id_recv.at[1], (opp, m)),
    ]
    c_copies = [None] + [
        remote(recv.at[0], recv.at[k], c_send.at[k], c_recv.at[k], (g, to_user[k])) for k in range(1, slots)
    ]
    a_copies = []
    for a in range(blocks):
        part = pl.ds(BLK * a, BLK)
        a_copies.append(remote(bank.at[part, :], prev.at[part, :], a_send.at[a], a_recv.at[a], (nxt, m)))

    column = jnp.full((1, 128), -1, jnp.int32)
    for k in range(slots):
        first = PREF + blocks * k
        member = m if k == 0 else to_owner[k]
        column = jnp.where((lane >= first) & (lane < first + blocks), blocks * member + lane - first, column)
    row_id = lax.broadcasted_iota(jnp.int32, sel.shape, 0)
    sel[...] = (row_id == column).astype(jnp.float32).astype(jnp.bfloat16)
    in_mask = ((lane >= PREF) & (lane < PREF + blocks * slots)).astype(jnp.float32)

    def build(k):
        bias = jnp.zeros((16, 128), jnp.float32)
        for t in range(3):
            bias = bias + jnp.dot(
                recv[k, half + 16 * t : half + 16 * t + 16, :],
                sel[128 * t : 128 * t + 128, :],
                preferred_element_type=jnp.float32,
            )
        bias = (bias - 1.0) * (-NEG) * in_mask
        for b in range(blocks):
            at = BLK * (b % (blocks // 2))
            part = recv[k, at : at + BLK, :].astype(jnp.float32)
            if b >= blocks // 2:
                part = pltpu.roll(part, PREF, 1)
            part = part * low
            hot = (lane == PREF + blocks * k + b).astype(jnp.float32)
            lhs[k, BLK * b : BLK * b + BLK, :] = (part + hot).astype(jnp.bfloat16)
            rhs[k, BLK * b : BLK * b + BLK, :] = (part + bias[b : b + 1, :]).astype(jnp.bfloat16)

    racc[...] = jnp.full_like(racc, NEG)
    cacc[...] = jnp.full_like(cacc, NEG)
    f_own[...] = jnp.full_like(f_own, NEG)
    f_prev[...] = jnp.full_like(f_prev, NEG)
    f_l[...] = jnp.full_like(f_l, NEG)

    own_copy.wait()
    for copy in id_copies:
        copy.wait_recv()
    id_local = pltpu.make_async_copy(ids, ids_s, loc_sem.at[2])
    id_local.start()
    id_local.wait()
    l_copies = []
    for j in range(cap):
        block = ids_s[2, g, j]
        picked = own[0:BLK, :]
        for b in range(1, blocks):
            picked = lax.select(block == b, own[BLK * b : BLK * b + BLK, :], picked)
        lsend[BLK * j : BLK * j + BLK, :] = picked
        part = pl.ds(BLK * j, BLK)
        l_copies.append(remote(lsend.at[part, :], lbuf.at[part, :], l_send.at[j], l_recv.at[j], (prv, m)))

    build(0)
    diag = jnp.where(
        lax.broadcasted_iota(jnp.int32, (BLK, BLK), 0) == lax.broadcasted_iota(jnp.int32, (BLK, BLK), 1), NEG, 0.0
    )

    for c in range(blocks):
        part = slice(BLK * c, BLK * c + BLK)
        s = dot_nt(lhs[0], rhs[0, part, :])
        for b in range(blocks):
            at = slice(BLK * b, BLK * b + BLK)
            x = s[at, :]
            if b == c:
                x = x + diag
            racc[0, at, :] = jnp.maximum(racc[0, at, :], x)

    def pair(a, b):
        for n in range(0, rows, 256):
            s = dot_nt(lhs[a], rhs[b, n : n + 256, :])
            racc[a] = jnp.maximum(racc[a], jnp.maximum(s[:, 0:128], s[:, 128:256]))
            cacc[b, :, n : n + 256] = jnp.maximum(
                cacc[b, :, n : n + 256], jnp.max(s.reshape(rows // 8, 8, 256), axis=0)
            )

    for b in range(1, slots):
        c_copies[b].wait_recv()
        build(b)

        def with_slot(a, carry, b=b):
            pair(a, b)
            return carry

        lax.fori_loop(0, b, with_slot, 0)

    def rows_to_lanes(x):
        return jnp.max(x.T.reshape(16, 8, 128), axis=0)

    def settle(k, carry):
        for b in range(blocks):
            at = slice(BLK * b, BLK * b + BLK)
            cacc[k, :, at] = jnp.maximum(cacc[k, :, at], rows_to_lanes(racc[k, at, :]))
        return carry

    lax.fori_loop(0, slots, settle, 0)
    b_copies = [None] + [
        remote(cacc.at[k], cret.at[k], b_send.at[k], b_recv.at[k], (g, to_owner[k])) for k in range(1, slots)
    ]

    def listed(which, group, b):
        count = ids_s[which, 4, group]
        hits = jnp.int32(0)
        for j in range(cap):
            hits = hits + ((ids_s[which, group, j] == b) & (j < count)).astype(jnp.int32)
        return hits

    mine = [listed(0, prv, b) for b in range(blocks)]
    theirs = [listed(1, g, b) for b in range(blocks)]
    live = [jnp.where(j < ids_s[1, 4, nxt], 0.0, NEG) for j in range(cap)]

    def tops(x):
        return jnp.max(x.reshape(BLK // 8, 8, BLK), axis=0)

    def own_with(a):
        at = slice(BLK * a, BLK * a + BLK)
        s = dot_nt(own[...], prev[at, :])
        top = f_prev[:, at]
        for b in range(blocks):
            here = slice(BLK * b, BLK * b + BLK)
            x = s[here, :] + jnp.where(mine[a] + theirs[b] > 0, 0.0, NEG)
            f_own[here, :] = jnp.maximum(f_own[here, :], x)
            top = jnp.maximum(top, tops(x))
        f_prev[:, at] = top

    def listed_with(a):
        at = slice(BLK * a, BLK * a + BLK)
        s = dot_nt(lbuf[...], prev[at, :])
        top = f_prev[:, at]
        for j in range(cap):
            here = slice(BLK * j, BLK * j + BLK)
            x = s[here, :] + live[j]
            f_l[here, :] = jnp.maximum(f_l[here, :], x)
            top = jnp.maximum(top, tops(x))
        f_prev[:, at] = top

    for a in range(blocks - 1):
        a_copies[a].wait_recv()
        own_with(a)
    for copy in l_copies:
        copy.wait_recv()
    for a in range(blocks - 1):
        listed_with(a)
    a_copies[blocks - 1].wait_recv()
    listed_with(blocks - 1)
    own_with(blocks - 1)
    for j in range(cap):
        r2s[j] = rows_to_lanes(f_l[BLK * j : BLK * j + BLK, :])
    r_copies = [
        remote(f_prev, r1, r_send.at[0], r_recv.at[0], (prv, m)),
        remote(r2s, r2, r_send.at[1], r_recv.at[1], (nxt, m)),
    ]

    best = cacc[0]
    for k in range(1, slots):
        b_copies[k].wait_recv()
        best = jnp.maximum(best, cret[k])
    coarse[...] = jnp.max(best, axis=0, keepdims=True)

    mine_best = [rows_to_lanes(f_own[BLK * b : BLK * b + BLK, :]) for b in range(blocks)]
    for copy in r_copies:
        copy.wait_recv()
    for b in range(blocks):
        at = slice(BLK * b, BLK * b + BLK)
        x = jnp.maximum(mine_best[b], r1[:, at])
        for j in range(cap):
            x = jnp.maximum(x, r2[j] + jnp.where(ids_s[2, g, j] == b, 0.0, NEG))
        fine[:, at] = jnp.max(x, axis=0, keepdims=True)

    for copy in id_copies + c_copies[1:] + a_copies + l_copies + b_copies[1:] + r_copies:
        copy.wait_send()


def solution(mesh):
    groups, members = mesh.shape["grp"], mesh.shape["mem"]
    cover = COVERS[members]
    slots = len(cover)

    def step(bank, pattern, pair_list, pair_count):
        rows, width = bank.shape
        blocks, group_blocks = pattern.shape
        cap = pair_list.shape[2]
        message = rows // 2 + 48
        bf16, f32, i32 = jnp.bfloat16, jnp.float32, jnp.int32
        vmem = pl.BlockSpec(memory_space=pltpu.VMEM)
        dma = pltpu.SemaphoreType.DMA
        coarse, fine = pl.pallas_call(
            functools.partial(kernel, cover, groups, members),
            out_shape=(jax.ShapeDtypeStruct((1, rows), f32), jax.ShapeDtypeStruct((1, rows), f32)),
            in_specs=[pl.BlockSpec(memory_space=pl.ANY), vmem, vmem, vmem],
            out_specs=(vmem, vmem),
            scratch_shapes=[
                pltpu.VMEM((rows, width), bf16),
                pltpu.VMEM((rows, 128), bf16),
                pltpu.VMEM((rows, width), bf16),
                pltpu.VMEM((cap * BLK, width), bf16),
                pltpu.VMEM((cap * BLK, width), bf16),
                pltpu.VMEM((slots, message, 128), bf16),
                pltpu.VMEM((slots, rows, 128), bf16),
                pltpu.VMEM((slots, rows, 128), bf16),
                pltpu.VMEM((slots, rows, 128), f32),
                pltpu.VMEM((slots, 8, rows), f32),
                pltpu.VMEM((slots, 8, rows), f32),
                pltpu.VMEM((16, 384), i32),
                pltpu.VMEM((384, 128), bf16),
                pltpu.VMEM((3, 8, 128), i32),
                pltpu.SMEM((3, 8, 128), i32),
                pltpu.VMEM((rows, 128), f32),
                pltpu.VMEM((8, rows), f32),
                pltpu.VMEM((cap * BLK, 128), f32),
                pltpu.VMEM((cap, 8, 128), f32),
                pltpu.VMEM((8, rows), f32),
                pltpu.VMEM((cap, 8, 128), f32),
                dma((3,)),
                dma((2,)), dma((2,)),
                dma((slots,)), dma((slots,)),
                dma((blocks,)), dma((blocks,)),
                dma((cap,)), dma((cap,)),
                dma((slots,)), dma((slots,)),
                dma((2,)), dma((2,)),
            ],
            compiler_params=pltpu.CompilerParams(
                collective_id=0, has_side_effects=True, vmem_limit_bytes=40 * 1024 * 1024
            ),
            name="pair_search",
        )(bank, pattern, pair_list, pair_count)
        return coarse.reshape(rows), fine.reshape(rows)

    return jax.shard_map(
        step,
        mesh=mesh,
        in_specs=(
            P(("grp", "mem"), None),
            P(("grp", "mem"), None),
            P(("grp", "mem"), None, None),
            P(("grp", "mem"), None),
        ),
        out_specs=(P(("grp", "mem")), P(("grp", "mem"))),
        check_vma=False,
    )
```

time: 290 us -> 55.3 us (0.19); the launches traced: 285 us -> 55.1 us
  matrix products: 151 us -> 0 us
  waiting for transfers between devices: 49.9 us -> 0 us
  Pallas kernels: 0 us -> 49.8 us
  local copies, waits for them, and re-layouts: 48.6 us -> 3.44 us
  between operations: 14.2 us -> 0.65 us
  blocking collectives: 8.88 us -> 0 us
  starting transfers between devices: 8.14 us -> 0 us
    dot_general x19 -> x0, matrix products: 151 us -> none  [the longest x3 124 us: one_tile(): lax.dot_general(block, cols, (((1,), (1,)), ((), ())), preferred_element_...]
    all_to_all x2 -> x0, waiting for transfers between devices: 49.9 us -> none  [the longest x1 45.9 us: per_device(): lax.all_to_all(outgoing, 'grp', split_axis=0, concat_axis=0, tiled=True)]
    pallas_call x0 -> x1, Pallas kernels: none -> 49.8 us  [step(): pl.pallas_call(functools.partial(kernel, cover, groups, members), out_sha...]
    broadcast_in_dim x19 -> x0, local copies, waits for them, and re-layouts: 21.9 us -> none  [the longest x3 21.8 us: one_tile(): jnp.broadcast_to(pblock[:, None, :, None] > 0, (blocks_per, BLK, count //...]
    reshape x3 -> x0, local copies, waits for them, and re-layouts: 16.8 us -> none  [the longest x1 16 us: per_device(): cols = lax.all_gather(packed, 'mem', axis=0, tiled=True).reshape(-1, PREF)]
    all_to_all x1 -> x0, blocking collectives: 8.88 us -> none  [per_device(): lax.all_to_all(asked, 'grp', split_axis=0, concat_axis=0, tiled=True)]
    all_to_all x2 -> x0, starting transfers between devices: 8.11 us -> none  [the longest x1 4.86 us: per_device(): lax.all_to_all(outgoing, 'grp', split_axis=0, concat_axis=0, tiled=True)]
    gather x1 -> x0, local copies, waits for them, and re-layouts: 4.19 us -> none  [per_device(): outgoing = local_blocks[ids_in]]
  transfers between devices with their start and end apart: 3 -> 0, of which waited for: 2 -> 0; matrix products, arithmetic and copies ran while one was open for 12% -> 0% of each run, Pallas kernels for 0% -> 0%
where the time goes in v1:
time: 55.3 us; the launch traced here: 55.1 us
  Pallas kernels  49.8 us (90%)
  local copies, waits for them, and re-layouts  3.44 us (6%)
  other arithmetic  1.21 us (2%)
  between operations  0.65 us (1%)
    pallas_call x1, Pallas kernels, step(): pl.pallas_call(functools.partial(kernel, cover, groups, members), out_sha...  49.8 us
    unnamed x8, local copies, waits for them, and re-layouts  3.44 us
    pallas_call x2, other arithmetic, step(): pl.pallas_call(functools.partial(kernel, cover, groups, members), out_sha...  1.21 us

profile of v1, /device:TPU:1, one launch (start us, length us, event | category | flops | bytes accessed | tf_op | source)
XLA Modules:
  0.0 55.1 jit_solution(12076985315137089936)
XLA Ops:
  0.6 0.0 copy-start
  0.6 1.4 %copy-done = bf16[768,1024]{1,0:T(8,128)(2,1)S(1)} copy-done((bf16[768,1024]{1,0:T(8,128)(2,1)S(1)}, bf16[768,1024]{1,0:T(8,128)(2,1)}, u32[]{:S(2)}) %copy-start) | copy-done | bytes 1572888
  2.0 0.0 copy-start.1
  2.0 0.7 %copy-done.1 = s32[6,384]{1,0:T(8,128)S(1)} copy-done((s32[6,384]{1,0:T(8,128)S(1)}, s32[6,384]{1,0:T(8,128)}, u32[]{:S(2)}) %copy-start.1) | copy-done | bytes 9240
  2.7 0.0 copy-start.2
  2.7 0.7 %copy-done.2 = s32[1,4,4]{2,1,0:T(4,128)S(1)} copy-done((s32[1,4,4]{2,1,0:T(4,128)S(1)}, s32[1,4,4]{2,1,0:T(4,128)}, u32[]{:S(2)}) %copy-start.2) | copy-done | bytes 88
  3.4 0.0 copy-start.3
  3.4 0.7 %copy-done.3 = s32[1,4]{1,0:T(1,128)S(1)} copy-done((s32[1,4]{1,0:T(1,128)S(1)}, s32[1,4]{1,0:T(1,128)}, u32[]{:S(2)}) %copy-start.3) | copy-done | bytes 40
  4.1 49.8 %pair_search.1 = (f32[1,768]{1,0:T(1,128)S(1)}, f32[1,768]{1,0:T(1,128)S(1)}) custom-call(bf16[768,1024]{1,0:T(8,128)(2,1)S(1)} %copy-done, s32[6,384]{1,0:T(8,128)S(1)} %copy-done.1, s32[1,4,4]{2,1,0:T(4,128)S(1)} %copy-done.2, s32[1,4]{1,0:T(1,128)S(1)} %copy-done.3), custom_call_target="tpu_custom_call" | custom-call | tf_op jit(solution)/shard_map/pair_search/pallas_call | solution.py:277
  53.9 0.6 %reduce = f32[768]{0:T(1024)} reduce(f32[1,768]{1,0:T(1,128)S(1)} %get-tuple-element.4, f32[]{:T(128)} %constant.3), dimensions={0}, to_apply=%get-tuple-element.4.reduce_sub_computation | reduce | bytes 6148 | tf_op jit(solution)/shard_map/pair_search/pallas_call | solution.py:277
  54.5 0.6 %reduce.1 = f32[768]{0:T(1024)} reduce(f32[1,768]{1,0:T(1,128)S(1)} %get-tuple-element.5, f32[]{:T(128)} %constant.3), dimensions={0}, to_apply=%get-tuple-element.5.reduce_sub_computation | reduce | bytes 6148 | tf_op jit(solution)/shard_map/pair_search/pallas_call | solution.py:277
Async XLA Ops:
  0.6 1.4 %copy-start = (bf16[768,1024]{1,0:T(8,128)(2,1)S(1)}, bf16[768,1024]{1,0:T(8,128)(2,1)}, u32[]{:S(2)}) copy-start(bf16[768,1024]{1,0:T(8,128)(2,1)} %bank.1) | copy-start | bytes 4718596
  2.0 0.7 %copy-start.1 = (s32[6,384]{1,0:T(8,128)S(1)}, s32[6,384]{1,0:T(8,128)}, u32[]{:S(2)}) copy-start(s32[6,384]{1,0:T(8,128)} %patt.1) | copy-start | bytes 27652
  2.7 0.7 %copy-start.2 = (s32[1,4,4]{2,1,0:T(4,128)S(1)}, s32[1,4,4]{2,1,0:T(4,128)}, u32[]{:S(2)}) copy-start(s32[1,4,4]{2,1,0:T(4,128)} %plist.1) | copy-start | bytes 196
  3.4 0.7 %copy-start.3 = (s32[1,4]{1,0:T(1,128)S(1)}, s32[1,4]{1,0:T(1,128)}, u32[]{:S(2)}) copy-start(s32[1,4]{1,0:T(1,128)} %pcount.1) | copy-start | bytes 52

commit v2 on v1

v2 whole, which is shorter than its diff:
```python
import functools

import jax
import jax.numpy as jnp
from jax import lax
from jax.experimental import pallas as pl
from jax.experimental.pallas import tpu as pltpu
from jax.sharding import PartitionSpec as P

PREF = 64
BLK = 128
NEG = -1e30
MESH = pl.DeviceIdType.MESH
COVERS = {64: (0, 1, 63, 58, 15, 41, 13, 4, 33), 4: (0, 1, 2)}


def dot_nt(a, b):
    return lax.dot_general(a, b, (((1,), (1,)), ((), ())), preferred_element_type=jnp.float32)


def kernel(
    cover, groups, members,
    bank, patt_in, plist_in, pcount_in,
    coarse, fine,
    patt, plist, pcount, own, pre, prev, lbuf, lsend, recv, lhs, rhs, racc, cacc, cret,
    pattpad, sel, ids, ids_s, f_own, f_prev, f_l, r2s, r1, r2,
    loc_sem, id_send, id_recv, c_send, c_recv, a_send, a_recv, l_send, l_recv, b_send, b_recv, r_send, r_recv, go_sem, mem_sem,
):
    g = lax.axis_index("grp")
    m = lax.axis_index("mem")
    core = lax.rem(m, 2)
    nxt = lax.rem(g + 1 + 2 * core, groups)
    prv = lax.rem(g + 3 - 2 * core, groups)
    opp = lax.rem(g + 2, groups)
    slots = len(cover)
    rows = own.shape[0]
    half = rows // 2
    blocks = rows // BLK
    cap = lbuf.shape[0] // BLK
    to_user = [None] + [lax.rem(m + members - d, members) for d in cover[1:]]
    to_owner = [None] + [lax.rem(m + d, members) for d in cover[1:]]

    pre_copy = pltpu.make_async_copy(bank.at[:, pl.ds(0, 128)], pre, loc_sem.at[0])
    pre_copy.start()
    small_copies = [
        pltpu.make_async_copy(src, dst, loc_sem.at[at])
        for src, dst, at in ((plist_in, plist, 3), (pcount_in, pcount, 4), (patt_in, patt, 5))
    ]
    for copy in small_copies:
        copy.start()
    own_copy = pltpu.make_async_copy(bank, own, loc_sem.at[1])
    own_copy.start()

    barrier = pltpu.get_barrier_semaphore()
    for step in range(1, groups):
        other = lax.rem(g + step, groups)

        @pl.when(other != 0)
        def _():
            pl.semaphore_signal(barrier, inc=1, device_id=(other, m), device_id_type=MESH)

    @pl.when(g != 0)
    def _():
        pl.semaphore_wait(barrier, groups - 1)

    @pl.when(g == 1)
    def _():
        pl.semaphore_signal(go_sem, inc=1, device_id=(0, m), device_id_type=MESH)

    @pl.when(g == 0)
    def _():
        pl.semaphore_wait(go_sem, 1)
        for k in range(1, slots):
            for other in (to_user[k], to_owner[k]):
                pl.semaphore_signal(barrier, inc=1, device_id=(0, other), device_id_type=MESH)

    def remote(src, dst, send, rcv, where):
        copy = pltpu.make_async_remote_copy(
            src_ref=src, dst_ref=dst, send_sem=send, recv_sem=rcv, device_id=where, device_id_type=MESH
        )
        copy.start()
        return copy

    ids[0] = jnp.zeros((8, 128), jnp.int32)
    pattpad[...] = jnp.zeros_like(pattpad)
    for copy in small_copies:
        copy.wait()
    ids[0, 0:4, 0:4] = plist[0]
    ids[0, 4:5, 0:4] = pcount[...]
    id_copies = [
        remote(ids.at[0], ids.at[1], id_send.at[0], id_recv.at[0], (nxt, m)),
        remote(ids.at[0], ids.at[2], id_send.at[1], id_recv.at[1], (opp, m)),
    ]
    a_copies = []
    for a in range(blocks):
        part = pl.ds(BLK * a, BLK)
        a_copies.append(remote(bank.at[part, :], prev.at[part, :], a_send.at[a], a_recv.at[a], (nxt, m)))

    lane = lax.broadcasted_iota(jnp.int32, (1, 128), 1)
    low = (lane < PREF).astype(jnp.float32)

    for t in range(3):
        pattpad[8 * t : 8 * t + blocks, :] = patt[:, 128 * t : 128 * t + 128]
    recv[0, half : half + 32, :] = pattpad[...].astype(jnp.float32).astype(jnp.bfloat16)
    pre_copy.wait()
    recv[0, 0:half, :] = (
        pre[0:half, :].astype(jnp.float32) * low
        + pltpu.roll(pre[half:rows, :].astype(jnp.float32) * low, PREF, 1)
    ).astype(jnp.bfloat16)

    own_copy.wait()
    for copy in id_copies:
        copy.wait_recv()
    id_local = pltpu.make_async_copy(ids, ids_s, loc_sem.at[2])
    id_local.start()
    id_local.wait()
    l_copies = []
    for j in range(cap):
        block = ids_s[2, g, j]
        picked = own[0:BLK, :]
        for b in range(1, blocks):
            picked = lax.select(block == b, own[BLK * b : BLK * b + BLK, :], picked)
        lsend[BLK * j : BLK * j + BLK, :] = picked
        part = pl.ds(BLK * j, BLK)
        l_copies.append(remote(lsend.at[part, :], lbuf.at[part, :], l_send.at[j], l_recv.at[j], (prv, m)))

    @pl.when(g == 0)
    def _():
        pl.semaphore_wait(barrier, 2 * (slots - 1))
        for other in range(1, groups):
            pl.semaphore_signal(mem_sem, inc=1, device_id=(other, m), device_id_type=MESH)

    @pl.when(g != 0)
    def _():
        pl.semaphore_wait(mem_sem, 1)

    c_copies = [None] + [
        remote(recv.at[0], recv.at[k], c_send.at[k], c_recv.at[k], (g, to_user[k])) for k in range(1, slots)
    ]

    column = jnp.full((1, 128), -1, jnp.int32)
    for k in range(slots):
        first = PREF + blocks * k
        member = m if k == 0 else to_owner[k]
        column = jnp.where((lane >= first) & (lane < first + blocks), blocks * member + lane - first, column)
    row_id = lax.broadcasted_iota(jnp.int32, sel.shape, 0)
    sel[...] = (row_id == column).astype(jnp.float32).astype(jnp.bfloat16)
    in_mask = ((lane >= PREF) & (lane < PREF + blocks * slots)).astype(jnp.float32)

    def build(k):
        parts = [
            jnp.dot(
                recv[k, half + 16 * (t // 2) : half + 16 * (t // 2) + 16, :],
                sel[128 * t : 128 * t + 128, :],
                preferred_element_type=jnp.float32,
            )
            for t in range(3)
        ]
        bias = parts[0][0:8] + parts[1][8:16] + parts[2][0:8]
        bias = (bias - 1.0) * (-NEG) * in_mask
        for b in range(blocks):
            at = BLK * (b % (blocks // 2))
            part = recv[k, at : at + BLK, :].astype(jnp.float32)
            if b >= blocks // 2:
                part = pltpu.roll(part, PREF, 1)
            part = part * low
            hot = (lane == PREF + blocks * k + b).astype(jnp.float32)
            lhs[k, BLK * b : BLK * b + BLK, :] = (part + hot).astype(jnp.bfloat16)
            rhs[k, BLK * b : BLK * b + BLK, :] = (part + bias[b : b + 1, :]).astype(jnp.bfloat16)

    f_own[...] = jnp.full_like(f_own, NEG)
    f_prev[...] = jnp.full_like(f_prev, NEG)
    f_l[...] = jnp.full_like(f_l, NEG)

    def tops(x):
        return jnp.max(x.reshape(BLK // 8, 8, BLK), axis=0)

    def rows_to_lanes(x):
        return jnp.max(x.T.reshape(16, 8, 128), axis=0)

    build(0)
    diag = jnp.where(
        lax.broadcasted_iota(jnp.int32, (BLK, BLK), 0) == lax.broadcasted_iota(jnp.int32, (BLK, BLK), 1), NEG, 0.0
    )
    for c in range(blocks):
        part = slice(BLK * c, BLK * c + BLK)
        s = dot_nt(lhs[0], rhs[0, part, :])
        top = jnp.full((8, BLK), NEG, jnp.float32)
        for b in range(blocks):
            x = s[BLK * b : BLK * b + BLK, :]
            if b == c:
                x = x + diag
            top = jnp.maximum(top, tops(x))
        cacc[0, :, part] = top

    done = set()

    def shard(b):
        c_copies[b].wait_recv()
        build(b)
        racc[...] = jnp.full_like(racc, NEG)
        for a in range(b):
            gap = (cover[a] - cover[b]) % members
            if min(gap, members - gap) in done:
                continue
            done.add(min(gap, members - gap))
            for n in range(0, rows, 256):
                s = dot_nt(lhs[b], rhs[a, n : n + 256, :])
                racc[...] = jnp.maximum(racc[...], jnp.maximum(s[:, 0:128], s[:, 128:256]))
                cacc[a, :, n : n + 256] = jnp.maximum(
                    cacc[a, :, n : n + 256], jnp.max(s.reshape(rows // 8, 8, 256), axis=0)
                )
        for c in range(blocks):
            at = slice(BLK * c, BLK * c + BLK)
            cacc[b, :, at] = rows_to_lanes(racc[at, :])

    def listed(which, group, b):
        count = ids_s[which, 4, group]
        hits = jnp.int32(0)
        for j in range(cap):
            hits = hits + ((ids_s[which, group, j] == b) & (j < count)).astype(jnp.int32)
        return hits

    mine = [listed(0, prv, b) for b in range(blocks)]
    theirs = [listed(1, g, b) for b in range(blocks)]
    live = [jnp.where(j < ids_s[1, 4, nxt], 0.0, NEG) for j in range(cap)]

    def own_with(first, last):
        for a in range(first, last):
            a_copies[a].wait_recv()
        s = dot_nt(own[...], prev[BLK * first : BLK * last, :])
        for a in range(first, last):
            at = slice(BLK * a, BLK * a + BLK)
            top = f_prev[:, at]
            for b in range(blocks):
                here = slice(BLK * b, BLK * b + BLK)
                x = s[here, BLK * (a - first) : BLK * (a - first) + BLK]
                x = x + jnp.where(mine[a] + theirs[b] > 0, 0.0, NEG)
                f_own[here, :] = jnp.maximum(f_own[here, :], x)
                top = jnp.maximum(top, tops(x))
            f_prev[:, at] = top

    def listed_with(first, last):
        s = dot_nt(lbuf[...], prev[BLK * first : BLK * last, :])
        for a in range(first, last):
            at = slice(BLK * a, BLK * a + BLK)
            top = f_prev[:, at]
            for j in range(cap):
                here = slice(BLK * j, BLK * j + BLK)
                x = s[here, BLK * (a - first) : BLK * (a - first) + BLK] + live[j]
                f_l[here, :] = jnp.maximum(f_l[here, :], x)
                top = jnp.maximum(top, tops(x))
            f_prev[:, at] = top

    early = {slots // 2: (0, 1), 3 * slots // 4: (1, 2)}
    for b in range(1, slots):
        shard(b)
        if b in early:
            own_with(*early[b])
    b_copies = [None] + [
        remote(cacc.at[k], cret.at[k], b_send.at[k], b_recv.at[k], (g, to_owner[k])) for k in range(1, slots)
    ]
    own_with(2, 4)
    for copy in l_copies:
        copy.wait_recv()
    listed_with(0, 4)
    own_with(4, 5)
    listed_with(4, 5)
    own_with(5, 6)
    listed_with(5, 6)
    for j in range(cap):
        r2s[j] = rows_to_lanes(f_l[BLK * j : BLK * j + BLK, :])
    r_copies = [
        remote(f_prev, r1, r_send.at[0], r_recv.at[0], (prv, m)),
        remote(r2s, r2, r_send.at[1], r_recv.at[1], (nxt, m)),
    ]

    best = cacc[0]
    for k in range(1, slots):
        b_copies[k].wait_recv()
        best = jnp.maximum(best, cret[k])
    coarse[...] = jnp.max(best, axis=0)

    mine_best = [rows_to_lanes(f_own[BLK * b : BLK * b + BLK, :]) for b in range(blocks)]
    for copy in r_copies:
        copy.wait_recv()
    for b in range(blocks):
        at = slice(BLK * b, BLK * b + BLK)
        x = jnp.maximum(mine_best[b], r1[:, at])
        for j in range(cap):
            x = jnp.maximum(x, r2[j] + jnp.where(ids_s[2, g, j] == b, 0.0, NEG))
        fine[at] = jnp.max(x, axis=0)

    for copy in id_copies + c_copies[1:] + a_copies + l_copies + b_copies[1:] + r_copies:
        copy.wait_send()


def solution(mesh):
    groups, members = mesh.shape["grp"], mesh.shape["mem"]
    cover = COVERS[members]
    slots = len(cover)

    def step(bank, pattern, pair_list, pair_count):
        rows, width = bank.shape
        blocks, group_blocks = pattern.shape
        cap = pair_list.shape[2]
        message = rows // 2 + 32
        bf16, f32, i32 = jnp.bfloat16, jnp.float32, jnp.int32
        vmem = pl.BlockSpec(memory_space=pltpu.VMEM)
        dma = pltpu.SemaphoreType.DMA
        coarse, fine = pl.pallas_call(
            functools.partial(kernel, cover, groups, members),
            out_shape=(jax.ShapeDtypeStruct((rows,), f32), jax.ShapeDtypeStruct((rows,), f32)),
            in_specs=[pl.BlockSpec(memory_space=pltpu.HBM)] * 4,
            out_specs=(vmem, vmem),
            scratch_shapes=[
                pltpu.VMEM(pattern.shape, i32),
                pltpu.VMEM(pair_list.shape, i32),
                pltpu.VMEM(pair_count.shape, i32),
                pltpu.VMEM((rows, width), bf16),
                pltpu.VMEM((rows, 128), bf16),
                pltpu.VMEM((rows, width), bf16),
                pltpu.VMEM((cap * BLK, width), bf16),
                pltpu.VMEM((cap * BLK, width), bf16),
                pltpu.VMEM((slots, message, 128), bf16),
                pltpu.VMEM((slots, rows, 128), bf16),
                pltpu.VMEM((slots, rows, 128), bf16),
                pltpu.VMEM((rows, 128), f32),
                pltpu.VMEM((slots, 8, rows), f32),
                pltpu.VMEM((slots, 8, rows), f32),
                pltpu.VMEM((32, 128), i32),
                pltpu.VMEM((384, 128), bf16),
                pltpu.VMEM((3, 8, 128), i32),
                pltpu.SMEM((3, 8, 128), i32),
                pltpu.VMEM((rows, 128), f32),
                pltpu.VMEM((8, rows), f32),
                pltpu.VMEM((cap * BLK, 128), f32),
                pltpu.VMEM((cap, 8, 128), f32),
                pltpu.VMEM((8, rows), f32),
                pltpu.VMEM((cap, 8, 128), f32),
                dma((6,)),
                dma((2,)), dma((2,)),
                dma((slots,)), dma((slots,)),
                dma((blocks,)), dma((blocks,)),
                dma((cap,)), dma((cap,)),
                dma((slots,)), dma((slots,)),
                dma((2,)), dma((2,)),
                pltpu.SemaphoreType.REGULAR,
                pltpu.SemaphoreType.REGULAR,
            ],
            compiler_params=pltpu.CompilerParams(
                collective_id=0, has_side_effects=True, vmem_limit_bytes=60 * 1024 * 1024
            ),
            name="pair_search",
        )(bank, pattern, pair_list, pair_count)
        return coarse, fine

    return jax.shard_map(
        step,
        mesh=mesh,
        in_specs=(
            P(("grp", "mem"), None),
            P(("grp", "mem"), None),
            P(("grp", "mem"), None, None),
            P(("grp", "mem"), None),
        ),
        out_specs=(P(("grp", "mem")), P(("grp", "mem"))),
        check_vma=False,
    )
```

time: 55.3 us -> 50.1 us (0.906)
  Pallas kernels: 49.8 us -> 46.8 us
  other arithmetic: 1.21 us -> 0 us
  local copies, waits for them, and re-layouts: 3.44 us -> 2.53 us
    pallas_call x1, Pallas kernels: 49.8 us -> 46.8 us  [step(): pl.pallas_call(functools.partial(kernel, cover, groups, members), out_sha...]
    pallas_call x2 -> x0, other arithmetic: 1.21 us -> none  [step(): pl.pallas_call(functools.partial(kernel, cover, groups, members), out_sha...]
    unnamed x8 -> x2, local copies, waits for them, and re-layouts: 3.44 us -> 2.53 us
where the time goes in v2:
time: 50.1 us; the launch traced here: 49.9 us
  Pallas kernels  46.8 us (93%)
  local copies, waits for them, and re-layouts  2.53 us (5%)
  between operations  0.64 us (1%)
    pallas_call x1, Pallas kernels, step(): pl.pallas_call(functools.partial(kernel, cover, groups, members), out_sha...  46.8 us
    unnamed x2, local copies, waits for them, and re-layouts  2.53 us

profile of v2, /device:TPU:1, one launch (start us, length us, event | category | flops | bytes accessed | tf_op | source)
XLA Modules:
  0.0 49.9 jit_solution(3392398415048857054)
XLA Ops:
  0.6 46.8 %pair_search.1 = (f32[768]{0:T(1024)}, f32[768]{0:T(1024)}) custom-call(bf16[768,1024]{1,0:T(8,128)(2,1)} %bank.1, s32[6,384]{1,0:T(8,128)} %patt_in.1, s32[1,4,4]{2,1,0:T(4,128)} %plist_in.1, s32[1,4]{1,0:T(1,128)} %pcount_in.1), custom_call_target="tpu_custom_call" | custom-call | tf_op jit(solution)/shard_map/pair_search/pallas_call | solution.py:311
  47.4 1.3 %copy.8 = f32[768]{0:T(1024)} copy(f32[768]{0:T(1024)} %get-tuple-element.4) | data formatting | bytes 6144
  48.7 1.3 %copy.9 = f32[768]{0:T(1024)} copy(f32[768]{0:T(1024)} %get-tuple-element.5) | data formatting | bytes 6144

commit v3 on v2

--- a/solution.py
+++ b/solution.py
@@ -11,17 +11,24 @@
 BLK = 128
 NEG = -1e30
 MESH = pl.DeviceIdType.MESH
-COVERS = {64: (0, 1, 63, 58, 15, 41, 13, 4, 33), 4: (0, 1, 2)}
+COVERS = {64: (0, 1, 2, 16, 5, 34, 14, 59, 42), 4: (0, 1, 2)}
 
 
 def dot_nt(a, b):
     return lax.dot_general(a, b, (((1,), (1,)), ((), ())), preferred_element_type=jnp.float32)
+
+
+def shifted(m, d, members):
+    if members != 64:
+        return lax.rem(m + d, members)
+    at = lax.rem(((m // 2) % 4) * 16 + (m // 8) * 2 + m % 2 + d, members)
+    return ((at // 2) % 8) * 8 + (at // 16) * 2 + at % 2
 
 
 def kernel(
     cover, groups, members,
     bank, patt_in, plist_in, pcount_in,
-    coarse, fine,
+    out,
     patt, plist, pcount, own, pre, prev, lbuf, lsend, recv, lhs, rhs, racc, cacc, cret,
     pattpad, sel, ids, ids_s, f_own, f_prev, f_l, r2s, r1, r2,
     loc_sem, id_send, id_recv, c_send, c_recv, a_send, a_recv, l_send, l_recv, b_send, b_recv, r_send, r_recv, go_sem, mem_sem,
@@ -37,8 +44,8 @@
     half = rows // 2
     blocks = rows // BLK
     cap = lbuf.shape[0] // BLK
-    to_user = [None] + [lax.rem(m + members - d, members) for d in cover[1:]]
-    to_owner = [None] + [lax.rem(m + d, members) for d in cover[1:]]
+    to_user = [None] + [shifted(m, members - d, members) for d in cover[1:]]
+    to_owner = [None] + [shifted(m, d, members) for d in cover[1:]]
 
     pre_copy = pltpu.make_async_copy(bank.at[:, pl.ds(0, 128)], pre, loc_sem.at[0])
     pre_copy.start()
@@ -67,17 +74,23 @@
     def _():
         pl.semaphore_signal(go_sem, inc=1, device_id=(0, m), device_id_type=MESH)
 
+    @pl.when(g == 1)
+    def _():
+        for k in range(1, slots):
+            for other in (to_user[k], to_owner[k]):
+                pl.semaphore_signal(barrier, inc=1, device_id=(0, other), device_id_type=MESH)
+
     @pl.when(g == 0)
     def _():
         pl.semaphore_wait(go_sem, 1)
-        for k in range(1, slots):
-            for other in (to_user[k], to_owner[k]):
-                pl.semaphore_signal(barrier, inc=1, device_id=(0, other), device_id_type=MESH)
-
-    def remote(src, dst, send, rcv, where):
-        copy = pltpu.make_async_remote_copy(
+
+    def planned(src, dst, send, rcv, where):
+        return pltpu.make_async_remote_copy(
             src_ref=src, dst_ref=dst, send_sem=send, recv_sem=rcv, device_id=where, device_id_type=MESH
         )
+
+    def remote(*args):
+        copy = planned(*args)
         copy.start()
         return copy
 
@@ -107,6 +120,27 @@
         pre[0:half, :].astype(jnp.float32) * low
         + pltpu.roll(pre[half:rows, :].astype(jnp.float32) * low, PREF, 1)
     ).astype(jnp.bfloat16)
+
+    c_copies = [None] + [
+        planned(recv.at[0], recv.at[k], c_send.at[k], c_recv.at[k], (g, to_user[k])) for k in range(1, slots)
+    ]
+
+    def send_prefixes():
+        @pl.when(g == 0)
+        def _():
+            pl.semaphore_wait(barrier, 2 * (slots - 1))
+            for other in range(1, groups):
+                pl.semaphore_signal(mem_sem, inc=1, device_id=(other, m), device_id_type=MESH)
+
+        @pl.when(g != 0)
+        def _():
+            pl.semaphore_wait(mem_sem, 1)
+
+        for copy in c_copies[1:]:
+            copy.start()
+
+    late = m // (members // 2)
+    pl.when(late == 1)(send_prefixes)
 
     own_copy.wait()
     for copy in id_copies:
@@ -124,19 +158,7 @@
         part = pl.ds(BLK * j, BLK)
         l_copies.append(remote(lsend.at[part, :], lbuf.at[part, :], l_send.at[j], l_recv.at[j], (prv, m)))
 
-    @pl.when(g == 0)
-    def _():
-        pl.semaphore_wait(barrier, 2 * (slots - 1))
-        for other in range(1, groups):
-            pl.semaphore_signal(mem_sem, inc=1, device_id=(other, m), device_id_type=MESH)
-
-    @pl.when(g != 0)
-    def _():
-        pl.semaphore_wait(mem_sem, 1)
-
-    c_copies = [None] + [
-        remote(recv.at[0], recv.at[k], c_send.at[k], c_recv.at[k], (g, to_user[k])) for k in range(1, slots)
-    ]
+    pl.when(late == 0)(send_prefixes)
 
     column = jnp.full((1, 128), -1, jnp.int32)
     for k in range(slots):
@@ -252,22 +274,15 @@
                 top = jnp.maximum(top, tops(x))
             f_prev[:, at] = top
 
-    early = {slots // 2: (0, 1), 3 * slots // 4: (1, 2)}
     for b in range(1, slots):
         shard(b)
-        if b in early:
-            own_with(*early[b])
     b_copies = [None] + [
         remote(cacc.at[k], cret.at[k], b_send.at[k], b_recv.at[k], (g, to_owner[k])) for k in range(1, slots)
     ]
-    own_with(2, 4)
+    own_with(0, blocks)
     for copy in l_copies:
         copy.wait_recv()
-    listed_with(0, 4)
-    own_with(4, 5)
-    listed_with(4, 5)
-    own_with(5, 6)
-    listed_with(5, 6)
+    listed_with(0, blocks)
     for j in range(cap):
         r2s[j] = rows_to_lanes(f_l[BLK * j : BLK * j + BLK, :])
     r_copies = [
@@ -279,7 +294,7 @@
     for k in range(1, slots):
         b_copies[k].wait_recv()
         best = jnp.maximum(best, cret[k])
-    coarse[...] = jnp.max(best, axis=0)
+    out[0:1, :] = jnp.max(best, axis=0, keepdims=True)
 
     mine_best = [rows_to_lanes(f_own[BLK * b : BLK * b + BLK, :]) for b in range(blocks)]
     for copy in r_copies:
@@ -289,7 +304,7 @@
         x = jnp.maximum(mine_best[b], r1[:, at])
         for j in range(cap):
             x = jnp.maximum(x, r2[j] + jnp.where(ids_s[2, g, j] == b, 0.0, NEG))
-        fine[at] = jnp.max(x, axis=0)
+        out[1:2, at] = jnp.max(x, axis=0, keepdims=True)
 
     for copy in id_copies + c_copies[1:] + a_copies + l_copies + b_copies[1:] + r_copies:
         copy.wait_send()
@@ -308,11 +323,11 @@
         bf16, f32, i32 = jnp.bfloat16, jnp.float32, jnp.int32
         vmem = pl.BlockSpec(memory_space=pltpu.VMEM)
         dma = pltpu.SemaphoreType.DMA
-        coarse, fine = pl.pallas_call(
+        out = pl.pallas_call(
             functools.partial(kernel, cover, groups, members),
-            out_shape=(jax.ShapeDtypeStruct((rows,), f32), jax.ShapeDtypeStruct((rows,), f32)),
+            out_shape=jax.ShapeDtypeStruct((2, rows), f32),
             in_specs=[pl.BlockSpec(memory_space=pltpu.HBM)] * 4,
-            out_specs=(vmem, vmem),
+            out_specs=vmem,
             scratch_shapes=[
                 pltpu.VMEM(pattern.shape, i32),
                 pltpu.VMEM(pair_list.shape, i32),
@@ -353,7 +368,7 @@
             ),
             name="pair_search",
         )(bank, pattern, pair_list, pair_count)
-        return coarse, fine
+        return out[0], out[1]
 
     return jax.shard_map(
         step,

time: 50.1 us -> 45.7 us (0.912)
  Pallas kernels: 46.8 us -> 43.5 us
  local copies, waits for them, and re-layouts: 2.53 us -> 1.38 us
    pallas_call x1, Pallas kernels: 46.8 us -> 43.5 us  [step(): pl.pallas_call(functools.partial(kernel, cover, groups, members), out_sha...]
    unnamed x2 -> x0, local copies, waits for them, and re-layouts: 2.53 us -> none
    slice x0 -> x1, local copies, waits for them, and re-layouts: none -> 1.38 us  [step(): return (out[0], out[1])]
where the time goes in v3:
time: 45.7 us; the launch traced here: 45.5 us
  Pallas kernels  43.5 us (95%)
  local copies, waits for them, and re-layouts  1.38 us (3%)
  between operations  0.64 us (1%)
    pallas_call x1, Pallas kernels, step(): pl.pallas_call(functools.partial(kernel, cover, groups, members), out_sha...  43.5 us
    slice x1, local copies, waits for them, and re-layouts, step(): return (out[0], out[1])  1.38 us

profile of v3, /device:TPU:1, one launch (start us, length us, event | category | flops | bytes accessed | tf_op | source)
XLA Modules:
  0.0 45.5 jit_solution(3293792172082922223)
XLA Ops:
  0.6 43.5 %pair_search.1 = f32[2,768]{1,0:T(2,128)} custom-call(bf16[768,1024]{1,0:T(8,128)(2,1)} %bank.1, s32[6,384]{1,0:T(8,128)} %patt_in.1, s32[1,4,4]{2,1,0:T(4,128)} %plist_in.1, s32[1,4]{1,0:T(1,128)} %pcount_in.1), custom_call_target="tpu_custom_call" | custom-call | tf_op jit(solution)/shard_map/pair_search/pallas_call | solution.py:326
  44.1 1.4 %slice_reduce_fusion = (f32[768]{0:T(1024)}, f32[768]{0:T(1024)}) fusion(f32[2,768]{1,0:T(2,128)} %pair_search.1), kind=kLoop, calls=%fused_computation | loop fusion | bytes 12288 | tf_op jit(solution)/shard_map/slice | solution.py:371

commit v4 on v3

--- a/solution.py
+++ b/solution.py
@@ -29,8 +29,8 @@
     cover, groups, members,
     bank, patt_in, plist_in, pcount_in,
     out,
-    patt, plist, pcount, own, pre, prev, lbuf, lsend, recv, lhs, rhs, racc, cacc, cret,
-    pattpad, sel, ids, ids_s, f_own, f_prev, f_l, r2s, r1, r2,
+    patt, plist, pcount, own, pre, prev, lbuf, lsend, recv, lhs, rhs, racc, cacc, crow, cret,
+    pattpad, sel, ids, ids_s, f_own, f_prev, f_row, f_l, r2s, r1, r2,
     loc_sem, id_send, id_recv, c_send, c_recv, a_send, a_recv, l_send, l_recv, b_send, b_recv, r_send, r_recv, go_sem, mem_sem,
 ):
     g = lax.axis_index("grp")
@@ -275,28 +275,38 @@
             f_prev[:, at] = top
 
     for b in range(1, slots):
+        if b == min(5, slots - 1):
+            pl.when(late == 0)(functools.partial(own_with, 0, 1))
         shard(b)
+    for k in range(1, slots):
+        crow[k] = jnp.max(cacc[k], axis=0, keepdims=True)
     b_copies = [None] + [
-        remote(cacc.at[k], cret.at[k], b_send.at[k], b_recv.at[k], (g, to_owner[k])) for k in range(1, slots)
-    ]
-    own_with(0, blocks)
+        remote(crow.at[k], cret.at[k], b_send.at[k], b_recv.at[k], (g, to_owner[k])) for k in range(1, slots)
+    ]
+    pl.when(late == 1)(functools.partial(own_with, 0, 1))
+    own_with(1, 4)
     for copy in l_copies:
         copy.wait_recv()
-    listed_with(0, blocks)
+    listed_with(0, 4)
+    own_with(4, blocks)
+    listed_with(4, blocks)
     for j in range(cap):
-        r2s[j] = rows_to_lanes(f_l[BLK * j : BLK * j + BLK, :])
+        r2s[j] = jnp.max(rows_to_lanes(f_l[BLK * j : BLK * j + BLK, :]), axis=0, keepdims=True)
+    f_row[...] = jnp.max(f_prev[...], axis=0, keepdims=True)
     r_copies = [
-        remote(f_prev, r1, r_send.at[0], r_recv.at[0], (prv, m)),
+        remote(f_row, r1, r_send.at[0], r_recv.at[0], (prv, m)),
         remote(r2s, r2, r_send.at[1], r_recv.at[1], (nxt, m)),
     ]
 
-    best = cacc[0]
+    best = jnp.max(cacc[0], axis=0, keepdims=True)
     for k in range(1, slots):
         b_copies[k].wait_recv()
         best = jnp.maximum(best, cret[k])
-    out[0:1, :] = jnp.max(best, axis=0, keepdims=True)
-
-    mine_best = [rows_to_lanes(f_own[BLK * b : BLK * b + BLK, :]) for b in range(blocks)]
+    out[0:1, :] = best
+
+    mine_best = [
+        jnp.max(rows_to_lanes(f_own[BLK * b : BLK * b + BLK, :]), axis=0, keepdims=True) for b in range(blocks)
+    ]
     for copy in r_copies:
         copy.wait_recv()
     for b in range(blocks):
@@ -304,7 +314,7 @@
         x = jnp.maximum(mine_best[b], r1[:, at])
         for j in range(cap):
             x = jnp.maximum(x, r2[j] + jnp.where(ids_s[2, g, j] == b, 0.0, NEG))
-        out[1:2, at] = jnp.max(x, axis=0, keepdims=True)
+        out[1:2, at] = x
 
     for copy in id_copies + c_copies[1:] + a_copies + l_copies + b_copies[1:] + r_copies:
         copy.wait_send()
@@ -342,17 +352,19 @@
                 pltpu.VMEM((slots, rows, 128), bf16),
                 pltpu.VMEM((rows, 128), f32),
                 pltpu.VMEM((slots, 8, rows), f32),
-                pltpu.VMEM((slots, 8, rows), f32),
+                pltpu.VMEM((slots, 1, rows), f32),
+                pltpu.VMEM((slots, 1, rows), f32),
                 pltpu.VMEM((32, 128), i32),
                 pltpu.VMEM((384, 128), bf16),
                 pltpu.VMEM((3, 8, 128), i32),
                 pltpu.SMEM((3, 8, 128), i32),
                 pltpu.VMEM((rows, 128), f32),
                 pltpu.VMEM((8, rows), f32),
+                pltpu.VMEM((1, rows), f32),
                 pltpu.VMEM((cap * BLK, 128), f32),
-                pltpu.VMEM((cap, 8, 128), f32),
-                pltpu.VMEM((8, rows), f32),
-                pltpu.VMEM((cap, 8, 128), f32),
+                pltpu.VMEM((cap, 1, 128), f32),
+                pltpu.VMEM((1, rows), f32),
+                pltpu.VMEM((cap, 1, 128), f32),
                 dma((6,)),
                 dma((2,)), dma((2,)),
                 dma((slots,)), dma((slots,)),

time: 45.7 us -> 45.1 us (0.987)
  Pallas kernels: 43.5 us -> 42.9 us
    pallas_call x1, Pallas kernels: 43.5 us -> 42.9 us  [step(): pl.pallas_call(functools.partial(kernel, cover, groups, members), out_sha...]
where the time goes in v4:
time: 45.1 us; the launch traced here: 44.9 us
  Pallas kernels  42.9 us (95%)
  local copies, waits for them, and re-layouts  1.38 us (3%)
  between operations  0.64 us (1%)
    pallas_call x1, Pallas kernels, step(): pl.pallas_call(functools.partial(kernel, cover, groups, members), out_sha...  42.9 us
    slice x1, local copies, waits for them, and re-layouts, step(): return (out[0], out[1])  1.38 us

profile of v4, /device:TPU:1, one launch (start us, length us, event | category | flops | bytes accessed | tf_op | source)
XLA Modules:
  0.0 44.9 jit_solution(10133956882328562513)
XLA Ops:
  0.6 42.9 %pair_search.1 = f32[2,768]{1,0:T(2,128)} custom-call(bf16[768,1024]{1,0:T(8,128)(2,1)} %bank.1, s32[6,384]{1,0:T(8,128)} %patt_in.1, s32[1,4,4]{2,1,0:T(4,128)} %plist_in.1, s32[1,4]{1,0:T(1,128)} %pcount_in.1), custom_call_target="tpu_custom_call" | custom-call | tf_op jit(solution)/shard_map/pair_search/pallas_call | solution.py:336
  43.6 1.4 %slice_reduce_fusion = (f32[768]{0:T(1024)}, f32[768]{0:T(1024)}) fusion(f32[2,768]{1,0:T(2,128)} %pair_search.1), kind=kLoop, calls=%fused_computation | loop fusion | bytes 12288 | tf_op jit(solution)/shard_map/slice | solution.py:383

commit v5 on v4

--- a/solution.py
+++ b/solution.py
@@ -11,7 +11,7 @@
 BLK = 128
 NEG = -1e30
 MESH = pl.DeviceIdType.MESH
-COVERS = {64: (0, 1, 2, 16, 5, 34, 14, 59, 42), 4: (0, 1, 2)}
+COVERS = {64: (0, 1, 2, 16, 5, 14, 34, 59, 42), 4: (0, 1, 2)}
 
 
 def dot_nt(a, b):

time: 45.1 us -> 45.1 us (level)
  no operation moved by 1% of the time
where the time goes in v5:
time: 45.1 us; the launch traced here: 44.9 us
  Pallas kernels  42.9 us (95%)
  local copies, waits for them, and re-layouts  1.38 us (3%)
  between operations  0.64 us (1%)
    pallas_call x1, Pallas kernels, step(): pl.pallas_call(functools.partial(kernel, cover, groups, members), out_sha...  42.9 us
    slice x1, local copies, waits for them, and re-layouts, step(): return (out[0], out[1])  1.38 us

profile of v5, /device:TPU:1, one launch (start us, length us, event | category | flops | bytes accessed | tf_op | source)
XLA Modules:
  0.0 44.9 jit_solution(10169082738885615319)
XLA Ops:
  0.6 42.9 %pair_search.1 = f32[2,768]{1,0:T(2,128)} custom-call(bf16[768,1024]{1,0:T(8,128)(2,1)} %bank.1, s32[6,384]{1,0:T(8,128)} %patt_in.1, s32[1,4,4]{2,1,0:T(4,128)} %plist_in.1, s32[1,4]{1,0:T(1,128)} %pcount_in.1), custom_call_target="tpu_custom_call" | custom-call | tf_op jit(solution)/shard_map/pair_search/pallas_call | solution.py:336
  43.6 1.4 %slice_reduce_fusion = (f32[768]{0:T(1024)}, f32[768]{0:T(1024)}) fusion(f32[2,768]{1,0:T(2,128)} %pair_search.1), kind=kLoop, calls=%fused_computation | loop fusion | bytes 12288 | tf_op jit(solution)/shard_map/slice | solution.py:383
